TPU v7x, 32 devices: a whole 2x2x4 slice. The times are simulated.
32 devices in a mesh: seq: 16 (over z, x, core), head: 2 (over y).
Axes of the slice: x: 2, y: 2, z: 4, core: 2. Of those that a mesh axis runs over, the one named last changes fastest.
Arguments:
- queries: bfloat16 [16384, 4096], P('seq', 'head'), may hold values from -0.5 to 0.5
- key_rows: bfloat16 [16384, 4096], P('seq', 'head'), may hold values from -6 to 6
- value_rows: bfloat16 [16384, 4096], P('seq', 'head'), may hold values from -6 to 6
- decay_rates: float32 [32], P('head'), as said below
- out_gain: float32 [4096], P('head'), may hold values from 0.5 to 1.5
Outputs:
- attended: bfloat16 [16384, 4096], P('seq', 'head')
Inputs may be any that keep to these rules, and one draw needn't show every extreme that they name: `decay_rates`: positive per-head decay rates.
All inputs are finite; a program needn't handle non-finite values.
Results may differ from a plain program's by a relative error of at most 0.0054.
Values sent between devices are 32-bit elements; how exact they have to be, the bound alone decides.
A program may use at most 128 MiB of HBM per device.

v0:
```python
import functools

import jax
import jax.numpy as jnp
from jax import lax
from jax.experimental import pallas as pl
from jax.experimental.pallas import tpu as pltpu
from jax.sharding import PartitionSpec as P

E = 128
BLOCK = 256
EPSILON = 1e-06
GROUP = 4
F32 = jnp.float32
BF16 = jnp.bfloat16


def dot(a, b, contract):
    return lax.dot_general(a, b, ((contract[:1], contract[1:]), ((), ())), preferred_element_type=F32)


def kernel(
    runs, ways,
    q_hbm, k_hbm, v_hbm, rates_hbm, out_hbm, sums_ref,
    rates, q_buf, k_buf, v_buf, o_buf, mix, acc, entering,
    s_loc, s_oth, c_tot, c_oth, p_in, p_out, e_mine, e_send, e_oth, ss_loc, ss_in,
    r_sem, q_sem, k_sem, v_sem, o_sem, s_ss, s_rs, c_ss, c_rs, p_ss, p_rs, e_ss, e_rs, n_ss, n_rs,
):
    heads, length = q_buf.shape[0], q_buf.shape[1]
    half = heads // 2
    blocks = length // BLOCK
    groups = runs // GROUP
    me = lax.axis_index("seq")
    way = lax.axis_index("head")
    core = lax.rem(me, 2)
    x = lax.rem(me // 2, 2)
    z = me // GROUP
    core_peer = me + 1 - 2 * core
    x_peer = me + 2 - 4 * x
    own0 = core * half
    oth0 = (1 - core) * half
    core_f = core.astype(F32)
    x_f = x.astype(F32)

    def load(hbm, buf, sem, h):
        return pltpu.make_async_copy(hbm.at[:, pl.ds(pl.multiple_of(h * E, E), E)], buf.at[h], sem.at[h])

    def store(h):
        return pltpu.make_async_copy(o_buf.at[h], out_hbm.at[:, pl.ds(pl.multiple_of(h * E, E), E)], o_sem.at[h])

    def remote(src, dst, ss, rs, seq, head):
        return pltpu.make_async_remote_copy(
            src_ref=src, dst_ref=dst, send_sem=ss, recv_sem=rs,
            device_id={"seq": seq, "head": head}, device_id_type=pl.DeviceIdType.MESH,
        )

    def state_copy(k):
        return remote(s_loc.at[oth0 + k], s_oth.at[k], s_ss.at[k], s_rs.at[k], core_peer, way)

    def chip_copy(k):
        return remote(c_tot.at[k], c_oth.at[k], c_ss.at[k], c_rs.at[k], x_peer, way)

    def chain_copy(k):
        up = lax.rem(me + GROUP, runs)
        return remote(p_out.at[k], p_in.at[k], p_ss.at[k], p_rs.at[k], up, way)

    def carry_copy(k):
        return remote(e_send.at[k], e_oth.at[k], e_ss.at[k], e_rs.at[k], core_peer, way)

    def norm_copy(d):
        return remote(ss_loc, ss_in.at[d - 1], n_ss.at[d - 1], n_rs.at[d - 1], me, lax.rem(way + d, ways))

    def start_states(k, c):
        for h in (own0 + k, oth0 + k):
            load(k_hbm, k_buf, k_sem, h).start()
            load(v_hbm, v_buf, v_sem, h).start()
        return c

    def start_queries(k, c):
        for h in (own0 + k, oth0 + k):
            load(q_hbm, q_buf, q_sem, h).start()
        return c

    rates_copy = pltpu.make_async_copy(rates_hbm, rates, r_sem)
    rates_copy.start()
    lax.fori_loop(0, half, start_states, 0)
    lax.fori_loop(0, half, start_queries, 0)

    barrier = pltpu.get_barrier_semaphore()

    def greet(seq, head):
        pl.semaphore_signal(
            barrier, inc=1, device_id={"seq": seq, "head": head}, device_id_type=pl.DeviceIdType.MESH
        )

    greet(core_peer, way)
    greet(x_peer, way)
    for d in range(1, ways):
        greet(me, lax.rem(way + d, ways))

    @pl.when(z > 0)
    def _():
        greet(me - GROUP, way)

    @pl.when(z < groups - 1)
    def _():
        greet(me + GROUP, way)

    @pl.when(z == 0)
    def _():
        p_in[...] = jnp.zeros_like(p_in)

    acc[...] = jnp.zeros_like(acc)
    rates_copy.wait()

    def power(rate, steps):
        return jnp.exp(jnp.full((1, E), -rate * steps, F32))

    row = lax.broadcasted_iota(jnp.int32, (BLOCK, E), 0).astype(F32)

    def local_states(k):
        pair = (oth0 + k, own0 + k)
        for h in pair:
            load(k_hbm, k_buf, k_sem, h).wait()
            load(v_hbm, v_buf, v_sem, h).wait()
        whole = [power(rates[h], float(BLOCK)) for h in pair]
        scale = [jnp.exp(-rates[h] * (BLOCK - 1 - row)) for h in pair]
        state = [None, None]
        for b in range(blocks):
            rows = pl.ds(b * BLOCK, BLOCK)
            for n, h in enumerate(pair):
                scaled = (k_buf[h, rows, :].astype(F32) * scale[n]).astype(BF16)
                part = dot(scaled, v_buf[h, rows, :], (0, 0))
                state[n] = part if b == 0 else state[n] * whole[n] + part
                if b < blocks - 1:
                    entering[h, b] = state[n]
                else:
                    s_loc[h] = state[n]

    def chip_total(k):
        rate = rates[own0 + k]
        state_copy(k).wait_recv()
        mine = power(rate, length * (1.0 - core_f))
        other = power(rate, length * core_f)
        c_tot[k] = mine * s_loc[own0 + k] + other * s_oth[k]
        chip_copy(k).start()

    def state_step(k, c):
        local_states(k)
        state_copy(k).start()
        chip_total(k - 1)
        return c

    local_states(0)
    pl.semaphore_wait(barrier, 2 + (ways - 1) + jnp.minimum(z, 1) + jnp.minimum(groups - 1 - z, 1))
    state_copy(0).start()
    lax.fori_loop(1, half, state_step, 0)
    chip_total(half - 1)

    small = E
    down = lax.broadcasted_iota(jnp.int32, (small, small), 0) - lax.broadcasted_iota(jnp.int32, (small, small), 1)
    down_f = down.astype(F32)

    def attend(k):
        pair = (own0 + k, oth0 + k)
        for h in pair:
            load(q_hbm, q_buf, q_sem, h).wait()
        near = [jnp.where(down >= 0, jnp.exp(-rates[h] * jnp.maximum(down_f, 0.0)), 0.0) for h in pair]
        far = [jnp.exp(-rates[h] * (down_f + small)) for h in pair]
        units = [(n, b) for n in range(2) for b in range(blocks)]

        def score(unit):
            rows = pl.ds(unit[1] * BLOCK, BLOCK)
            return dot(q_buf[pair[unit[0]], rows, :], k_buf[pair[unit[0]], rows, :], (1, 1))

        ahead = score(units[0])
        for at, (n, b) in enumerate(units):
            scores = ahead
            if at + 1 < len(units):
                ahead = score(units[at + 1])
            vals = v_buf[pair[n], pl.ds(b * BLOCK, BLOCK), :]
            top = (scores[:small, :small] * near[n]).astype(BF16)
            low = jnp.concatenate(
                [(scores[small:, :small] * far[n]).astype(BF16), (scores[small:, small:] * near[n]).astype(BF16)],
                axis=1,
            )
            mix[pair[n], pl.ds(b * BLOCK, small), :] = dot(top, vals[:small], (1, 0))
            mix[pair[n], pl.ds(b * BLOCK + small, small), :] = dot(low, vals, (1, 0))

    def chain(k):
        rate = rates[own0 + k]
        chip_copy(k).wait_recv()

        @pl.when(z > 0)
        def _():
            chain_copy(k).wait_recv()

        before = p_in[k]
        other = c_oth[k]
        two = 2.0 * length

        @pl.when(z < groups - 1)
        def _():
            total = power(rate, two * (1.0 - x_f)) * c_tot[k] + power(rate, two * x_f) * other
            p_out[k] = power(rate, 2.0 * two) * before + total
            chain_copy(k).start()

        chip = power(rate, two * x_f) * before + x_f * other

        @pl.when(core == 0)
        def _():
            e_mine[k] = chip
            e_send[k] = power(rate, float(length)) * chip + s_loc[own0 + k]

        @pl.when(core == 1)
        def _():
            e_mine[k] = power(rate, float(length)) * chip + s_oth[k]
            e_send[k] = chip

        carry_copy(k).start()

    def finish(k):
        pair = (own0 + k, oth0 + k)
        carry_copy(k).wait_recv()
        carry = (e_mine[k], e_oth[k])
        scale = [jnp.exp(-rates[h] * (row + 1.0)) for h in pair]
        for b in range(blocks):
            rows = pl.ds(b * BLOCK, BLOCK)
            squares = acc[rows, :]
            for n, h in enumerate(pair):
                state = carry[n]
                if b > 0:
                    state = power(rates[h], float(b * BLOCK)) * state + entering[h, b - 1]
                mixed = mix[h, rows, :] + scale[n] * dot(q_buf[h, rows, :], state.astype(BF16), (1, 0))
                o_buf[h, rows, :] = mixed.astype(BF16)
                squares = squares + mixed * mixed
            acc[rows, :] = squares
        for h in pair:
            store(h).start()

    top_lag = min((3 * (groups - 1) + 1) // 2, half)
    lag = jnp.minimum((3 * z + 1) // 2, half)

    def step(i, c):
        @pl.when(i < half)
        def _():
            attend(i)

        def turn(n, c):
            k = 2 * (i - lag) + n

            @pl.when(jnp.logical_and(k >= 0, k < half))
            def _():
                chain(k)

            j = 2 * (i - top_lag) + n - 1

            @pl.when(jnp.logical_and(j >= 0, j < half))
            def _():
                finish(j)

            return c

        return lax.fori_loop(0, 2, turn, c)

    lax.fori_loop(0, max(half, top_lag + half // 2 + 1), step, 0)

    slabs = length // E
    for g in range(slabs):
        ss_loc[pl.ds(g, 1), :] = jnp.sum(acc[pl.ds(g * E, E), :].T, axis=0, keepdims=True)
    for d in range(1, ways):
        norm_copy(d).start()
    for d in range(1, ways):
        norm_copy(d).wait_recv()
    sums = ss_loc[...]
    for d in range(1, ways):
        sums = sums + ss_in[d - 1]
    sums_ref[...] = sums

    def drain(k, c):
        state_copy(k).wait_send()
        chip_copy(k).wait_send()
        carry_copy(k).wait_send()

        @pl.when(z < groups - 1)
        def _():
            chain_copy(k).wait_send()

        store(k).wait()
        store(half + k).wait()
        return c

    lax.fori_loop(0, half, drain, 0)
    for d in range(1, ways):
        norm_copy(d).wait_send()


def normalise(width, mixed_ref, sums_ref, gain_ref, out_ref):
    slabs = mixed_ref.shape[0] // E
    for t in range(slabs):
        sums = sums_ref[pl.ds(pl.program_id(0) * slabs + t, 1), :]
        inverse = jnp.broadcast_to(lax.rsqrt(sums / width + EPSILON), (E, E)).T
        rows = pl.ds(t * E, E)
        for h in range(mixed_ref.shape[1] // E):
            cols = pl.ds(h * E, E)
            out_ref[rows, cols] = (mixed_ref[rows, cols].astype(F32) * inverse * gain_ref[:, cols]).astype(BF16)


def body(runs, ways, queries, key_rows, value_rows, decay_rates, out_gain):
    length, columns = queries.shape
    heads = decay_rates.shape[0]
    half = heads // 2
    blocks = length // BLOCK
    dma = pltpu.SemaphoreType.DMA
    states = [pltpu.VMEM((half, E, E), F32)]
    sems = [dma((half,))]
    any_spec = pl.BlockSpec(memory_space=pl.ANY)
    sums_shape = (length // E, E)
    mixed, sums = pl.pallas_call(
        functools.partial(kernel, runs, ways),
        out_shape=(jax.ShapeDtypeStruct(queries.shape, BF16), jax.ShapeDtypeStruct(sums_shape, F32)),
        in_specs=[pl.BlockSpec(memory_space=pltpu.HBM)] * 4,
        out_specs=(any_spec, pl.BlockSpec(memory_space=pltpu.VMEM)),
        scratch_shapes=[pltpu.SMEM((heads,), F32)]
        + [pltpu.VMEM((heads, length, E), BF16)] * 4
        + [
            pltpu.VMEM((heads, length, E), F32),
            pltpu.VMEM((length, E), F32),
            pltpu.VMEM((heads, blocks - 1, E, E), F32),
            pltpu.VMEM((heads, E, E), F32),
        ]
        + states * 8
        + [pltpu.VMEM(sums_shape, F32), pltpu.VMEM((max(ways - 1, 1),) + sums_shape, F32)]
        + [dma]
        + [dma((heads,))] * 4
        + sems * 8
        + [dma((max(ways - 1, 1),))] * 2,
        compiler_params=pltpu.CompilerParams(
            collective_id=0, has_side_effects=True, vmem_limit_bytes=44 * 1024 * 1024
        ),
        cost_estimate=pl.CostEstimate(
            flops=12 * length * BLOCK * heads * E, bytes_accessed=8 * length * heads * E, transcendentals=0
        ),
    )(queries, key_rows, value_rows, decay_rates)
    tile = BLOCK
    return pl.pallas_call(
        functools.partial(normalise, float(heads * ways * E)),
        out_shape=jax.ShapeDtypeStruct(queries.shape, BF16),
        grid=(length // tile,),
        in_specs=[
            pl.BlockSpec((tile, columns), lambda i: (i, 0)),
            pl.BlockSpec(sums_shape, lambda i: (0, 0)),
            pl.BlockSpec((1, columns), lambda i: (0, 0)),
        ],
        out_specs=pl.BlockSpec((tile, columns), lambda i: (i, 0)),
        cost_estimate=pl.CostEstimate(
            flops=3 * length * columns, bytes_accessed=4 * length * columns, transcendentals=0
        ),
    )(mixed, sums, out_gain.reshape(1, columns))


def solution(mesh):
    placed = (P("seq", "head"), P("seq", "head"), P("seq", "head"), P("head"), P("head"))
    return jax.shard_map(
        functools.partial(body, mesh.shape["seq"], mesh.shape["head"]),
        mesh=mesh, in_specs=placed, out_specs=P("seq", "head"), check_vma=False,
    )
```

profile of v0, /device:TPU:24, one launch (start us, length us, event | category | flops | bytes accessed | tf_op | source)
XLA Modules:
  0.0 44.6 jit_solution(17622110987626713860)
XLA Ops:
  0.0 0.0 copy-start.2
  0.0 2.2 %copy-done.2 = bf16[1024,2048]{1,0:T(8,128)(2,1)S(1)} copy-done((bf16[1024,2048]{1,0:T(8,128)(2,1)S(1)}, bf16[1024,2048]{1,0:T(8,128)(2,1)}, u32[]{:S(2)}) %copy-start.2) | copy-done | bytes 4194328
  2.2 0.0 copy-start.3
  2.2 0.7 %copy-done.3 = f32[16]{0:T(128)S(1)} copy-done((f32[16]{0:T(128)S(1)}, f32[16]{0:T(128)}, u32[]{:S(2)}) %copy-start.3) | copy-done | bytes 88
  2.8 34.0 %shard_map.55 = (bf16[1024,2048]{1,0:T(8,128)(2,1)S(1)}, f32[8,128]{1,0:T(8,128)S(1)}) custom-call(bf16[1024,2048]{1,0:T(8,128)(2,1)S(1)} %copy-done.2, bf16[1024,2048]{1,0:T(8,128)(2,1)} %k_hbm.1, bf16[1024,2048]{1,0:T(8,128)(2,1)} %v_hbm.1, f32[16]{0:T(128)S(1)} %copy-done.3), custom_call_target="tpu_custom_call" | custom-call | flops 6442450944 | bytes 16777216 | tf_op jit(solution)/shard_map/pallas_call | solution.py:319
  36.8 0.0 copy-start
  36.8 1.9 %copy-done = bf16[1024,2048]{1,0:T(8,128)(2,1)} copy-done((bf16[1024,2048]{1,0:T(8,128)(2,1)}, bf16[1024,2048]{1,0:T(8,128)(2,1)S(1)}, u32[]{:S(2)}) %copy-start) | copy-done | bytes 4194328
  38.8 0.0 copy-start.1
  38.8 0.6 %copy-done.1 = f32[8,128]{1,0:T(8,128)} copy-done((f32[8,128]{1,0:T(8,128)}, f32[8,128]{1,0:T(8,128)S(1)}, u32[]{:S(2)}) %copy-start.1) | copy-done | bytes 4120
  39.3 5.3 %shard_map.56 = bf16[1024,2048]{1,0:T(8,128)(2,1)} custom-call(bf16[1024,2048]{1,0:T(8,128)(2,1)} %copy-done, f32[8,128]{1,0:T(8,128)} %copy-done.1, f32[1,2048]{1,0:T(1,128)} %bitcast.1), custom_call_target="tpu_custom_call" | custom-call | flops 6291456 | bytes 8388608 | tf_op jit(solution)/shard_map/pallas_call | solution.py:346
Async XLA Ops:
  0.0 2.2 %copy-start.2 = (bf16[1024,2048]{1,0:T(8,128)(2,1)S(1)}, bf16[1024,2048]{1,0:T(8,128)(2,1)}, u32[]{:S(2)}) copy-start(bf16[1024,2048]{1,0:T(8,128)(2,1)} %q_hbm.1) | copy-start | bytes 12582916
  2.2 0.7 %copy-start.3 = (f32[16]{0:T(128)S(1)}, f32[16]{0:T(128)}, u32[]{:S(2)}) copy-start(f32[16]{0:T(128)} %rates_hbm.1) | copy-start | bytes 196
  36.8 1.9 %copy-start = (bf16[1024,2048]{1,0:T(8,128)(2,1)}, bf16[1024,2048]{1,0:T(8,128)(2,1)S(1)}, u32[]{:S(2)}) copy-start(bf16[1024,2048]{1,0:T(8,128)(2,1)S(1)} %get-tuple-element.7.mixed_ref) | copy-start | bytes 12582916
  38.8 0.6 %copy-start.1 = (f32[8,128]{1,0:T(8,128)}, f32[8,128]{1,0:T(8,128)S(1)}, u32[]{:S(2)}) copy-start(f32[8,128]{1,0:T(8,128)S(1)} %get-tuple-element.8.sums_ref) | copy-start | bytes 12292
where the time goes:
time: 44.9 us; the launch traced here: 44.6 us
  Pallas kernels  39.2 us (87%)
  local copies, waits for them, and re-layouts  5.36 us (12%)
    pallas_call x1, Pallas kernels, body(): pl.pallas_call(functools.partial(kernel, runs, ways), out_shape=(jax.Shap...  34 us
    unnamed x8, local copies, waits for them, and re-layouts  5.36 us
    pallas_call x1, Pallas kernels, body(): pl.pallas_call(functools.partial(normalise, float(heads * ways * E)), out...  5.26 us

commit v1 on v0

--- a/solution.py
+++ b/solution.py
@@ -21,10 +21,10 @@
 
 def kernel(
     runs, ways,
-    q_hbm, k_hbm, v_hbm, rates_hbm, out_hbm, sums_ref,
-    rates, q_buf, k_buf, v_buf, o_buf, mix, acc, entering,
+    q_hbm, k_hbm, v_hbm, rates_hbm, mix, sums_ref,
+    rates, q_buf, k_buf, v_buf, acc, entering,
     s_loc, s_oth, c_tot, c_oth, p_in, p_out, e_mine, e_send, e_oth, ss_loc, ss_in,
-    r_sem, q_sem, k_sem, v_sem, o_sem, s_ss, s_rs, c_ss, c_rs, p_ss, p_rs, e_ss, e_rs, n_ss, n_rs,
+    r_sem, q_sem, k_sem, v_sem, s_ss, s_rs, c_ss, c_rs, p_ss, p_rs, e_ss, e_rs, n_ss, n_rs,
 ):
     heads, length = q_buf.shape[0], q_buf.shape[1]
     half = heads // 2
@@ -44,9 +44,6 @@
 
     def load(hbm, buf, sem, h):
         return pltpu.make_async_copy(hbm.at[:, pl.ds(pl.multiple_of(h * E, E), E)], buf.at[h], sem.at[h])
-
-    def store(h):
-        return pltpu.make_async_copy(o_buf.at[h], out_hbm.at[:, pl.ds(pl.multiple_of(h * E, E), E)], o_sem.at[h])
 
     def remote(src, dst, ss, rs, seq, head):
         return pltpu.make_async_remote_copy(
@@ -232,11 +229,9 @@
                 if b > 0:
                     state = power(rates[h], float(b * BLOCK)) * state + entering[h, b - 1]
                 mixed = mix[h, rows, :] + scale[n] * dot(q_buf[h, rows, :], state.astype(BF16), (1, 0))
-                o_buf[h, rows, :] = mixed.astype(BF16)
+                mix[h, rows, :] = mixed
                 squares = squares + mixed * mixed
             acc[rows, :] = squares
-        for h in pair:
-            store(h).start()
 
     top_lag = min((3 * (groups - 1) + 1) // 2, half)
     lag = jnp.minimum((3 * z + 1) // 2, half)
@@ -286,8 +281,6 @@
         def _():
             chain_copy(k).wait_send()
 
-        store(k).wait()
-        store(half + k).wait()
         return c
 
     lax.fori_loop(0, half, drain, 0)
@@ -296,14 +289,14 @@
 
 
 def normalise(width, mixed_ref, sums_ref, gain_ref, out_ref):
-    slabs = mixed_ref.shape[0] // E
+    slabs = mixed_ref.shape[1] // E
     for t in range(slabs):
         sums = sums_ref[pl.ds(pl.program_id(0) * slabs + t, 1), :]
         inverse = jnp.broadcast_to(lax.rsqrt(sums / width + EPSILON), (E, E)).T
         rows = pl.ds(t * E, E)
-        for h in range(mixed_ref.shape[1] // E):
+        for h in range(mixed_ref.shape[0]):
             cols = pl.ds(h * E, E)
-            out_ref[rows, cols] = (mixed_ref[rows, cols].astype(F32) * inverse * gain_ref[:, cols]).astype(BF16)
+            out_ref[rows, cols] = (mixed_ref[h, rows, :] * inverse * gain_ref[:, cols]).astype(BF16)
 
 
 def body(runs, ways, queries, key_rows, value_rows, decay_rates, out_gain):
@@ -314,17 +307,17 @@
     dma = pltpu.SemaphoreType.DMA
     states = [pltpu.VMEM((half, E, E), F32)]
     sems = [dma((half,))]
-    any_spec = pl.BlockSpec(memory_space=pl.ANY)
+    fixed = [pltpu.with_memory_space_constraint(a, pltpu.HBM) for a in (queries, key_rows, value_rows, decay_rates)]
+    gain = pltpu.with_memory_space_constraint(out_gain.reshape(1, columns), pltpu.HBM)
     sums_shape = (length // E, E)
     mixed, sums = pl.pallas_call(
         functools.partial(kernel, runs, ways),
-        out_shape=(jax.ShapeDtypeStruct(queries.shape, BF16), jax.ShapeDtypeStruct(sums_shape, F32)),
+        out_shape=(jax.ShapeDtypeStruct((heads, length, E), F32), jax.ShapeDtypeStruct(sums_shape, F32)),
         in_specs=[pl.BlockSpec(memory_space=pltpu.HBM)] * 4,
-        out_specs=(any_spec, pl.BlockSpec(memory_space=pltpu.VMEM)),
+        out_specs=(pl.BlockSpec(memory_space=pltpu.VMEM),) * 2,
         scratch_shapes=[pltpu.SMEM((heads,), F32)]
-        + [pltpu.VMEM((heads, length, E), BF16)] * 4
+        + [pltpu.VMEM((heads, length, E), BF16)] * 3
         + [
-            pltpu.VMEM((heads, length, E), F32),
             pltpu.VMEM((length, E), F32),
             pltpu.VMEM((heads, blocks - 1, E, E), F32),
             pltpu.VMEM((heads, E, E), F32),
@@ -332,31 +325,32 @@
         + states * 8
         + [pltpu.VMEM(sums_shape, F32), pltpu.VMEM((max(ways - 1, 1),) + sums_shape, F32)]
         + [dma]
-        + [dma((heads,))] * 4
+        + [dma((heads,))] * 3
         + sems * 8
         + [dma((max(ways - 1, 1),))] * 2,
         compiler_params=pltpu.CompilerParams(
-            collective_id=0, has_side_effects=True, vmem_limit_bytes=44 * 1024 * 1024
+            collective_id=0, has_side_effects=True, vmem_limit_bytes=40 * 1024 * 1024
         ),
         cost_estimate=pl.CostEstimate(
             flops=12 * length * BLOCK * heads * E, bytes_accessed=8 * length * heads * E, transcendentals=0
         ),
-    )(queries, key_rows, value_rows, decay_rates)
+    )(*fixed)
     tile = BLOCK
     return pl.pallas_call(
         functools.partial(normalise, float(heads * ways * E)),
         out_shape=jax.ShapeDtypeStruct(queries.shape, BF16),
         grid=(length // tile,),
         in_specs=[
-            pl.BlockSpec((tile, columns), lambda i: (i, 0)),
+            pl.BlockSpec((heads, tile, E), lambda i: (0, i, 0)),
             pl.BlockSpec(sums_shape, lambda i: (0, 0)),
             pl.BlockSpec((1, columns), lambda i: (0, 0)),
         ],
         out_specs=pl.BlockSpec((tile, columns), lambda i: (i, 0)),
+        compiler_params=pltpu.CompilerParams(vmem_limit_bytes=16 * 1024 * 1024),
         cost_estimate=pl.CostEstimate(
             flops=3 * length * columns, bytes_accessed=4 * length * columns, transcendentals=0
         ),
-    )(mixed, sums, out_gain.reshape(1, columns))
+    )(mixed, sums, gain)
 
 
 def solution(mesh):

time: 44.9 us -> 36.6 us (0.82)
  local copies, waits for them, and re-layouts: 5.36 us -> 0 us
  Pallas kernels: 39.2 us -> 36.4 us
    unnamed x8 -> x0, local copies, waits for them, and re-layouts: 5.36 us -> none
    pallas_call x1, Pallas kernels: 34 us -> 32.5 us  [body(): pl.pallas_call(functools.partial(kernel, runs, ways), out_shape=(jax.Shap...]
    pallas_call x1, Pallas kernels: 5.26 us -> 3.91 us  [body(): pl.pallas_call(functools.partial(normalise, float(heads * ways * E)), out...]
where the time goes in v1:
time: 36.6 us; the launch traced here: 36.4 us
  Pallas kernels  36.4 us (99%)
    pallas_call x1, Pallas kernels, body(): pl.pallas_call(functools.partial(kernel, runs, ways), out_shape=(jax.Shap...  32.5 us
    pallas_call x1, Pallas kernels, body(): pl.pallas_call(functools.partial(normalise, float(heads * ways * E)), out...  3.91 us

profile of v1, /device:TPU:24, one launch (start us, length us, event | category | flops | bytes accessed | tf_op | source)
XLA Modules:
  0.0 36.4 jit_solution(17316778245178246069)
XLA Ops:
  0.0 32.5 %shard_map.55 = (f32[16,1024,128]{2,1,0:T(8,128)S(1)}, f32[8,128]{1,0:T(8,128)S(1)}) custom-call(bf16[1024,2048]{1,0:T(8,128)(2,1)} %q_hbm.1, bf16[1024,2048]{1,0:T(8,128)(2,1)} %k_hbm.1, bf16[1024,2048]{1,0:T(8,128)(2,1)} %v_hbm.1, f32[16]{0:T(128)} %rates_hbm.1), custom_call_target="tpu_custom_call" | custom-call | flops 6442450944 | bytes 16777216 | tf_op jit(solution)/shard_map/pallas_call | solution.py:313
  32.5 3.9 %shard_map.56 = bf16[1024,2048]{1,0:T(8,128)(2,1)} custom-call(f32[16,1024,128]{2,1,0:T(8,128)S(1)} %get-tuple-element.7.mixed_ref, f32[8,128]{1,0:T(8,128)S(1)} %get-tuple-element.8.sums_ref, f32[1,2048]{1,0:T(1,128)} %bitcast.1), custom_call_target="tpu_custom_call" | custom-call | flops 6291456 | bytes 8388608 | tf_op jit(solution)/shard_map/pallas_call | solution.py:339

commit v2 on v1

--- a/solution.py
+++ b/solution.py
@@ -113,7 +113,20 @@
     def power(rate, steps):
         return jnp.exp(jnp.full((1, E), -rate * steps, F32))
 
-    row = lax.broadcasted_iota(jnp.int32, (BLOCK, E), 0).astype(F32)
+    row = lax.broadcasted_iota(jnp.int32, (8, E), 0).astype(F32)
+
+    def rising(rate):
+        column = jnp.exp(-rate * (row + 1.0))
+        while column.shape[0] < BLOCK:
+            column = jnp.concatenate([column, column * power(rate, float(column.shape[0]))], axis=0)
+        return column
+
+    def falling(rate):
+        column = jnp.exp(-rate * (7.0 - row))
+        while column.shape[0] < BLOCK:
+            column = jnp.concatenate([column * power(rate, float(column.shape[0])), column], axis=0)
+        return column
+
 
     def local_states(k):
         pair = (oth0 + k, own0 + k)
@@ -121,7 +134,7 @@
             load(k_hbm, k_buf, k_sem, h).wait()
             load(v_hbm, v_buf, v_sem, h).wait()
         whole = [power(rates[h], float(BLOCK)) for h in pair]
-        scale = [jnp.exp(-rates[h] * (BLOCK - 1 - row)) for h in pair]
+        scale = [falling(rates[h]) for h in pair]
         state = [None, None]
         for b in range(blocks):
             rows = pl.ds(b * BLOCK, BLOCK)
@@ -157,13 +170,15 @@
     small = E
     down = lax.broadcasted_iota(jnp.int32, (small, small), 0) - lax.broadcasted_iota(jnp.int32, (small, small), 1)
     down_f = down.astype(F32)
+    left = (small - 1) - lax.broadcasted_iota(jnp.int32, (1, small), 1).astype(F32)
+    blank = jnp.zeros((small, small), BF16)
 
     def attend(k):
         pair = (own0 + k, oth0 + k)
         for h in pair:
             load(q_hbm, q_buf, q_sem, h).wait()
         near = [jnp.where(down >= 0, jnp.exp(-rates[h] * jnp.maximum(down_f, 0.0)), 0.0) for h in pair]
-        far = [jnp.exp(-rates[h] * (down_f + small)) for h in pair]
+        far = [rising(rates[h])[:small] * jnp.exp(-rates[h] * left) for h in pair]
         units = [(n, b) for n in range(2) for b in range(blocks)]
 
         def score(unit):
@@ -176,13 +191,12 @@
             if at + 1 < len(units):
                 ahead = score(units[at + 1])
             vals = v_buf[pair[n], pl.ds(b * BLOCK, BLOCK), :]
-            top = (scores[:small, :small] * near[n]).astype(BF16)
+            top = jnp.concatenate([(scores[:small, :small] * near[n]).astype(BF16), blank], axis=1)
             low = jnp.concatenate(
                 [(scores[small:, :small] * far[n]).astype(BF16), (scores[small:, small:] * near[n]).astype(BF16)],
                 axis=1,
             )
-            mix[pair[n], pl.ds(b * BLOCK, small), :] = dot(top, vals[:small], (1, 0))
-            mix[pair[n], pl.ds(b * BLOCK + small, small), :] = dot(low, vals, (1, 0))
+            mix[pair[n], pl.ds(b * BLOCK, BLOCK), :] = dot(jnp.concatenate([top, low], axis=0), vals, (1, 0))
 
     def chain(k):
         rate = rates[own0 + k]
@@ -220,7 +234,7 @@
         pair = (own0 + k, oth0 + k)
         carry_copy(k).wait_recv()
         carry = (e_mine[k], e_oth[k])
-        scale = [jnp.exp(-rates[h] * (row + 1.0)) for h in pair]
+        scale = [rising(rates[h]) for h in pair]
         for b in range(blocks):
             rows = pl.ds(b * BLOCK, BLOCK)
             squares = acc[rows, :]
@@ -288,15 +302,33 @@
         norm_copy(d).wait_send()
 
 
-def normalise(width, mixed_ref, sums_ref, gain_ref, out_ref):
+def normalise(width, mixed_ref, sums_ref, gain_hbm, out_hbm, gain, ready, gain_sem, out_sem):
     slabs = mixed_ref.shape[1] // E
-    for t in range(slabs):
-        sums = sums_ref[pl.ds(pl.program_id(0) * slabs + t, 1), :]
-        inverse = jnp.broadcast_to(lax.rsqrt(sums / width + EPSILON), (E, E)).T
-        rows = pl.ds(t * E, E)
+    fetch = pltpu.make_async_copy(gain_hbm, gain, gain_sem)
+    fetch.start()
+
+    def put(t):
+        rows = pl.ds(pl.multiple_of(t * E, E), E)
+        return pltpu.make_async_copy(ready.at[rows], out_hbm.at[rows], out_sem.at[t])
+
+    fetch.wait()
+
+    def slab(t, c):
+        inverse = jnp.broadcast_to(lax.rsqrt(sums_ref[pl.ds(t, 1), :] / width + EPSILON), (E, E)).T
+        rows = pl.ds(pl.multiple_of(t * E, E), E)
         for h in range(mixed_ref.shape[0]):
             cols = pl.ds(h * E, E)
-            out_ref[rows, cols] = (mixed_ref[h, rows, :] * inverse * gain_ref[:, cols]).astype(BF16)
+            ready[rows, cols] = (mixed_ref[h, rows, :] * inverse * gain[:, cols]).astype(BF16)
+        put(t).start()
+        return c
+
+    lax.fori_loop(0, slabs, slab, 0)
+
+    def drain(t, c):
+        put(t).wait()
+        return c
+
+    lax.fori_loop(0, slabs, drain, 0)
 
 
 def body(runs, ways, queries, key_rows, value_rows, decay_rates, out_gain):
@@ -335,17 +367,17 @@
             flops=12 * length * BLOCK * heads * E, bytes_accessed=8 * length * heads * E, transcendentals=0
         ),
     )(*fixed)
-    tile = BLOCK
     return pl.pallas_call(
         functools.partial(normalise, float(heads * ways * E)),
         out_shape=jax.ShapeDtypeStruct(queries.shape, BF16),
-        grid=(length // tile,),
-        in_specs=[
-            pl.BlockSpec((heads, tile, E), lambda i: (0, i, 0)),
-            pl.BlockSpec(sums_shape, lambda i: (0, 0)),
-            pl.BlockSpec((1, columns), lambda i: (0, 0)),
+        in_specs=[pl.BlockSpec(memory_space=pltpu.VMEM)] * 2 + [pl.BlockSpec(memory_space=pltpu.HBM)],
+        out_specs=pl.BlockSpec(memory_space=pltpu.HBM),
+        scratch_shapes=[
+            pltpu.VMEM((1, columns), F32),
+            pltpu.VMEM(queries.shape, BF16),
+            dma,
+            dma((length // E,)),
         ],
-        out_specs=pl.BlockSpec((tile, columns), lambda i: (i, 0)),
         compiler_params=pltpu.CompilerParams(vmem_limit_bytes=16 * 1024 * 1024),
         cost_estimate=pl.CostEstimate(
             flops=3 * length * columns, bytes_accessed=4 * length * columns, transcendentals=0

time: 36.6 us -> 35.7 us (0.975)
  Pallas kernels: 36.4 us -> 35.3 us
    pallas_call x1, Pallas kernels: 3.91 us -> 3.15 us  [body(): pl.pallas_call(functools.partial(normalise, float(heads * ways * E)), out...]
    pallas_call x1, Pallas kernels: 32.5 us -> 32.1 us  [body(): pl.pallas_call(functools.partial(kernel, runs, ways), out_shape=(jax.Shap...]
where the time goes in v2:
time: 35.7 us; the launch traced here: 35.3 us
  Pallas kernels  35.3 us (99%)
    pallas_call x1, Pallas kernels, body(): pl.pallas_call(functools.partial(kernel, runs, ways), out_shape=(jax.Shap...  32.1 us
    pallas_call x1, Pallas kernels, body(): pl.pallas_call(functools.partial(normalise, float(heads * ways * E)), out...  3.15 us

profile of v2, /device:TPU:24, one launch (start us, length us, event | category | flops | bytes accessed | tf_op | source)
XLA Modules:
  0.0 35.3 jit_solution(10255326151267602227)
XLA Ops:
  0.0 32.1 %shard_map.55 = (f32[16,1024,128]{2,1,0:T(8,128)S(1)}, f32[8,128]{1,0:T(8,128)S(1)}) custom-call(bf16[1024,2048]{1,0:T(8,128)(2,1)} %q_hbm.1, bf16[1024,2048]{1,0:T(8,128)(2,1)} %k_hbm.1, bf16[1024,2048]{1,0:T(8,128)(2,1)} %v_hbm.1, f32[16]{0:T(128)} %rates_hbm.1), custom_call_target="tpu_custom_call" | custom-call | flops 6442450944 | bytes 16777216 | tf_op jit(solution)/shard_map/pallas_call | solution.py:345
  32.1 3.2 %shard_map.56 = bf16[1024,2048]{1,0:T(8,128)(2,1)} custom-call(f32[16,1024,128]{2,1,0:T(8,128)S(1)} %get-tuple-element.7.mixed_ref, f32[8,128]{1,0:T(8,128)S(1)} %get-tuple-element.8.sums_ref, f32[1,2048]{1,0:T(1,128)} %bitcast.1), custom_call_target="tpu_custom_call" | custom-call | flops 6291456 | bytes 8388608 | tf_op jit(solution)/shard_map/pallas_call | solution.py:370
